TPU v7x, 128 devices: a whole 4x4x4 slice. The times are simulated.
128 devices in a mesh: tm: 32 (over y, x, core), hid: 4 (over z).
Axes of the slice: x: 4, y: 4, z: 4, core: 2. Of those that a mesh axis runs over, the one named last changes fastest.
Arguments:
- gate_inputs: bfloat16 [8192, 3, 4096], P('tm', None, 'hid'), may hold values from -6 to 16
- recurrent: bfloat16 [3, 4096, 4096], P(None, None, 'hid'), may hold values from -0.09375 to 0.09375
- initial_state: float32 [4096], P('hid'), may hold values from -0.9 to 0.9
- guess: bfloat16 [8192, 4096], P('tm', 'hid'), may hold values from -0.8984375 to 0.8984375
Outputs:
- trajectory: bfloat16 [8192, 4096], P('tm', 'hid')
All inputs are finite; a program needn't handle non-finite values.
Results may differ from a plain program's by a relative error of at most 0.003.
Values may be sent and summed in bfloat16 or wider, within the bound.
A program may use at most 128 MiB of HBM per device.

v0:
```python
import jax
import jax.numpy as jnp
from jax import lax
from jax.sharding import PartitionSpec as P

ITERS = 2


def from_behind(x, axis, by):
    size = lax.axis_size(axis)
    pairs = [(i, i + by) for i in range(size) if 0 <= i + by < size]
    return lax.ppermute(x, axis, pairs)


def prefix(value, axis, join, neutral):
    count, mine = (lax.axis_size(axis), lax.axis_index(axis))
    pieces = jax.tree.map(lambda part: lax.all_gather(part, axis), value)
    total = jax.tree.map(
        lambda part, zero: jnp.full_like(part, 0) + jnp.asarray(zero, part.dtype), value, neutral
    )

    def turn(position, total):
        longer = join(total, jax.tree.map(lambda part: part[position], pieces))
        return jax.tree.map(lambda new, old: jnp.where(position < mine, new, old), longer, total)

    return lax.fori_loop(0, count - 1, turn, total)


def compose(earlier, later):
    earlier_gain, earlier_shift = earlier
    later_gain, later_shift = later
    return (later_gain * earlier_gain, later_gain * earlier_shift + later_shift)


def boundary_row(states):
    return from_behind(states[-1], "tm", 1)


def per_device(gate_inputs, recurrent, initial_state, guess):
    rows = gate_inputs.shape[0]
    own = recurrent.shape[2]
    hid_index = lax.axis_index("hid")
    time_index = lax.axis_index("tm")
    own_block = lax.dynamic_slice_in_dim(recurrent, hid_index * own, own, 1)
    diagonal = jnp.diagonal(own_block, axis1=1, axis2=2).astype(jnp.float32)
    inputs = gate_inputs.astype(jnp.float32)
    states = guess.astype(jnp.float32)
    entering = initial_state
    for step in range(ITERS):
        incoming = jnp.where(time_index == 0, initial_state, boundary_row(states))
        previous = jnp.concatenate([incoming[None, :], states[:-1]], axis=0)
        empty = jnp.zeros((rows, 3, own), jnp.float32)
        piece = lax.all_gather(previous.astype(jnp.bfloat16), "hid", axis=1, tiled=True)
        weight_rows = lax.slice_in_dim(recurrent, 0, piece.shape[1], axis=1)
        total = empty + jnp.einsum(
            "tk,gko->tgo", piece, weight_rows, preferred_element_type=jnp.float32
        )
        memory = total[:, 2]
        update = jax.nn.sigmoid(inputs[:, 0] + total[:, 0])
        reset = jax.nn.sigmoid(inputs[:, 1] + total[:, 1])
        candidate = jnp.tanh(inputs[:, 2] + reset * memory)
        target = (1.0 - update) * candidate + update * previous
        slope = (
            update * (1.0 - update) * diagonal[0] * (previous - candidate)
            + (1.0 - update)
            * (1.0 - candidate * candidate)
            * (reset * (1.0 - reset) * diagonal[1] * memory + reset * diagonal[2])
            + update
        )
        offset = target - slope * previous
        gains, shifts = lax.associative_scan(compose, (slope, offset), axis=0)
        identity = (jnp.ones((own,), jnp.float32), jnp.zeros((own,), jnp.float32))
        before_gain, before_shift = prefix((gains[-1], shifts[-1]), "tm", compose, identity)
        entering = before_gain * initial_state + before_shift
        states = gains * entering[None, :] + shifts
    return states.astype(jnp.bfloat16)


def solution(mesh):
    in_specs = (P("tm", None, "hid"), P(None, None, "hid"), P("hid"), P("tm", "hid"))
    out_specs = P("tm", "hid")
    return jax.shard_map(
        per_device, mesh=mesh, in_specs=in_specs, out_specs=out_specs, check_vma=False
    )
```

profile of v0, /device:TPU:1, one launch (start us, length us, event | category | flops | bytes accessed | tf_op | source)
XLA Modules:
  0.0 480.0 jit_solution(14330377499558345989)
XLA Ops:
  7.3 4.5 collective-permute-start
  14.1 6.1 %constant_dynamic-slice_fusion.4 = bf16[3,1024,1024]{2,1,0:T(8,128)(2,1)} fusion(bf16[3,4096,1024]{2,1,0:T(8,128)(2,1)} %param.9, s32[]{:T(128)S(6)} %select_n.77), kind=kLoop, calls=%fused_computation.194 | loop fusion | bytes 12582916 | tf_op jit(solution)/shard_map/dynamic_slice | solution.py:44
  20.3 11.5 %copy.12 = bf16[3,1024,1024]{2,0,1:T(4,128)(2,1)} copy(bf16[3,1024,1024]{2,1,0:T(8,128)(2,1)} %constant_dynamic-slice_fusion.4) | data formatting | bytes 12582912
  33.6 12.5 %gather_fusion = bf16[1024,3]{0,1:T(4,128)(2,1)S(1)} fusion(bf16[3,1024,1024]{2,0,1:T(4,128)(2,1)} %copy.12, s32[1024]{0:T(1024)S(1)} %bitcast.117), kind=kCustom, calls=%fused_computation | custom fusion | bytes 20480 | tf_op jit(solution)/shard_map/jit(diagonal)/gather | solution.py:45
  47.6 12.3 %fusion.2 = f32[256,3,1024]{2,0,1:T(8,128)S(1)} fusion(bf16[3,4096,1024]{2,1,0:T(8,128)(2,1)} %param.9, bf16[256,4096]{1,0:T(8,128)(2,1)} %all-gather.7.cloned.1.call-done), kind=kOutput, calls=%fused_computation.11 | convolution fusion | flops 6442450944 | bytes 30408704 | tf_op jit(solution)/shard_map/tk,gko->tgo/dot_general | solution.py:55
  62.4 3.3 slice.539
  65.7 3.2 slice.540
  68.9 3.2 slice.576
  72.2 3.2 slice.577
  147.0 3.3 slice.538
  150.3 3.3 slice.611
  190.3 4.6 pad.227
  203.0 2.9 add_multiply_fusion.3
  206.8 4.6 pad.226
  212.2 25.9 %all-gather.1 = f32[32,1,1024]{2,1,0:T(1,128)S(1)} all-gather(f32[1,1,1024]{2,1,0:T(1,128)S(1)} %add_bitcast_fusion.2), channel_id=1, replica_groups=mesh['tm'=32,'hid'=4] {'tm'}, dimensions={0}, use_global_device_ids=true | all-gather | bytes 135168 | tf_op jit(solution)/shard_map/all_gather | solution.py:17
  238.1 4.6 pad.211
  244.6 4.7 pad.210
  250.1 23.1 %all-gather = f32[32,1,1024]{2,1,0:T(1,128)S(1)} all-gather(f32[1,1,1024]{2,1,0:T(1,128)S(1)} %add_bitcast_fusion.3), channel_id=1, replica_groups=mesh['tm'=32,'hid'=4] {'tm'}, dimensions={0}, use_global_device_ids=true | all-gather | bytes 135168 | tf_op jit(solution)/shard_map/all_gather | solution.py:17
  281.8 33.1 %all-gather.9.cloned.1.call-done = bf16[256,4096]{1,0:T(8,128)(2,1)} async-done(((bf16[256,1024]{1,0:T(8,128)(2,1)}), bf16[256,4096]{1,0:T(8,128)(2,1)}) %all-gather.9.cloned.1.call-update) | async-done | bytes 2097168 | tf_op jit(solution)/shard_map/all_gather | solution.py:53
  314.9 12.3 %fusion = f32[256,3,1024]{2,0,1:T(8,128)S(1)} fusion(bf16[3,4096,1024]{2,1,0:T(8,128)(2,1)} %param.9, bf16[256,4096]{1,0:T(8,128)(2,1)} %all-gather.9.cloned.1.call-done), kind=kOutput, calls=%fused_computation.9 | convolution fusion | flops 6442450944 | bytes 30408704 | tf_op jit(solution)/shard_map/tk,gko->tgo/dot_general | solution.py:55
  334.0 3.2 slice.657
  410.4 25.1 %all-gather.3 = f32[32,1,1024]{2,1,0:T(1,128)S(1)} all-gather(f32[1,1,1024]{2,1,0:T(1,128)S(1)} %add_bitcast_fusion), channel_id=1, replica_groups=mesh['tm'=32,'hid'=4] {'tm'}, dimensions={0}, use_global_device_ids=true | all-gather | bytes 135168 | tf_op jit(solution)/shard_map/all_gather | solution.py:17
  439.5 4.6 pad.242
  444.9 23.9 %all-gather.2 = f32[32,1,1024]{2,1,0:T(1,128)S(1)} all-gather(f32[1,1,1024]{2,1,0:T(1,128)S(1)} %add_bitcast_fusion.1), channel_id=1, replica_groups=mesh['tm'=32,'hid'=4] {'tm'}, dimensions={0}, use_global_device_ids=true | all-gather | bytes 135168 | tf_op jit(solution)/shard_map/all_gather | solution.py:17
  (492 shorter events, 227.4 us)
Async XLA Ops:
  6.5 41.0 %all-gather.7.cloned.1.call-start = ((), (), s32[]{:S(2)}) async-start(), calls=%async_computation | async-start | bytes 2621440 | tf_op jit(solution)/shard_map/all_gather | solution.py:53
  7.3 5.7 %collective-permute-start = (f32[1024]{0:T(1024)S(1)}, f32[1024]{0:T(1024)S(1)}, u32[]{:S(2)}, u32[]{:S(2)}) collective-permute-start(f32[1024]{0:T(1024)S(1)} %bitcast.138), channel_id=1, source_target_pairs={{0,4},{4,8},{8,12},{12,16},{16,20},{20,24},{24,28},{28,32},{32,36}... | collective-permute-start | bytes 12296 | tf_op jit(solution)/shard_map/ppermute | solution.py:12
  14.1 300.8 %all-gather.9.cloned.1.call-start = ((), (), s32[]{:S(2)}) async-start(), calls=%async_computation.1 | async-start | bytes 2621440 | tf_op jit(solution)/shard_map/all_gather | solution.py:53
  46.2 13.6 %copy-start.20 = (f32[1,1024]{1,0:T(1,128)}, f32[1,1024]{1,0:T(1,128)S(1)}, u32[]{:S(2)}) copy-start(f32[1,1024]{1,0:T(1,128)S(1)} %get-tuple-element.364) | copy-start | bytes 12292
  136.5 19.7 %copy-start.13 = (f32[7,1024]{1,0:T(8,128)S(1)}, f32[7,1024]{1,0:T(8,128)}, u32[]{:S(2)}) copy-start(f32[7,1024]{1,0:T(8,128)} %slice.554) | copy-start | bytes 86020
  136.5 19.7 %copy-start.14 = (f32[7,1024]{1,0:T(8,128)S(1)}, f32[7,1024]{1,0:T(8,128)}, u32[]{:S(2)}) copy-start(f32[7,1024]{1,0:T(8,128)} %slice.603) | copy-start | bytes 86020
  136.5 21.8 %copy-start.10 = (f32[15,1024]{1,0:T(8,128)S(1)}, f32[15,1024]{1,0:T(8,128)}, u32[]{:S(2)}) copy-start(f32[15,1024]{1,0:T(8,128)} %slice.550) | copy-start | bytes 184324
  140.8 14.9 %copy-start.27 = (f32[2,1024]{1,0:T(2,128)S(1)}, f32[2,1024]{1,0:T(2,128)}, u32[]{:S(2)}) copy-start(f32[2,1024]{1,0:T(2,128)} %get-tuple-element.379) | copy-start | bytes 24580
  140.8 14.9 %copy-start.26 = (f32[2,1024]{1,0:T(2,128)S(1)}, f32[2,1024]{1,0:T(2,128)}, u32[]{:S(2)}) copy-start(f32[2,1024]{1,0:T(2,128)} %get-tuple-element.378) | copy-start | bytes 24580
  140.8 15.0 %copy-start.45 = (f32[1,1024]{1,0:T(1,128)S(1)}, f32[1,1024]{1,0:T(1,128)}, u32[]{:S(2)}) copy-start(f32[1,1024]{1,0:T(1,128)} %get-tuple-element.357) | copy-start | bytes 12292
  140.8 15.0 %copy-start.46 = (f32[1,1024]{1,0:T(1,128)S(1)}, f32[1,1024]{1,0:T(1,128)}, u32[]{:S(2)}) copy-start(f32[1,1024]{1,0:T(1,128)} %get-tuple-element.358) | copy-start | bytes 12292
  140.8 15.0 %copy-start.47 = (f32[1,1024]{1,0:T(1,128)S(1)}, f32[1,1024]{1,0:T(1,128)}, u32[]{:S(2)}) copy-start(f32[1,1024]{1,0:T(1,128)} %get-tuple-element.359) | copy-start | bytes 12292
  140.8 15.0 %copy-start.48 = (f32[1,1024]{1,0:T(1,128)S(1)}, f32[1,1024]{1,0:T(1,128)}, u32[]{:S(2)}) copy-start(f32[1,1024]{1,0:T(1,128)} %get-tuple-element.360) | copy-start | bytes 12292
  140.8 15.1 %copy-start.18 = (f32[3,1024]{1,0:T(4,128)S(1)}, f32[3,1024]{1,0:T(4,128)}, u32[]{:S(2)}) copy-start(f32[3,1024]{1,0:T(4,128)} %slice.558) | copy-start | bytes 36868
  140.8 15.1 %copy-start.19 = (f32[3,1024]{1,0:T(4,128)S(1)}, f32[3,1024]{1,0:T(4,128)}, u32[]{:S(2)}) copy-start(f32[3,1024]{1,0:T(4,128)} %slice.601) | copy-start | bytes 36868
  140.8 15.1 %copy-start.40 = (f32[1,1024]{1,0:T(1,128)S(1)}, f32[1,1024]{1,0:T(1,128)}, u32[]{:S(2)}) copy-start(f32[1,1024]{1,0:T(1,128)} %slice.738) | copy-start | bytes 12292
  140.9 15.2 %copy-start.39 = (f32[1,1024]{1,0:T(1,128)S(1)}, f32[1,1024]{1,0:T(1,128)}, u32[]{:S(2)}) copy-start(f32[1,1024]{1,0:T(1,128)} %slice.712) | copy-start | bytes 12292
  183.1 16.2 %copy-start.6 = (f32[64,1024]{1,0:T(8,128)S(1)}, f32[64,1024]{1,0:T(8,128)}, u32[]{:S(2)}) copy-start(f32[64,1024]{1,0:T(8,128)} %add.477) | copy-start | bytes 786436
  205.9 36.8 %copy-start.28 = (f32[1,1024]{1,0:T(1,128)S(1)}, f32[1,1024]{1,0:T(1,128)}, u32[]{:S(2)}) copy-start(f32[1,1024]{1,0:T(1,128)} %slice.707) | copy-start | bytes 12292
  206.8 68.3 %copy-start.17 = (f32[1024]{0:T(1024)S(1)}, f32[1024]{0:T(1024)}, u32[]{:S(2)}) copy-start(f32[1024]{0:T(1024)} %param.10) | copy-start | bytes 12292
  277.8 3.1 collective-permute-start.1
  281.8 45.4 %copy-start.21 = (f32[1,1024]{1,0:T(1,128)S(1)}, f32[1,1024]{1,0:T(1,128)}, u32[]{:S(2)}) copy-start(f32[1,1024]{1,0:T(1,128)} %copy-done.20) | copy-start | bytes 12292
  281.8 45.4 %copy-start.23 = (f32[1,1024]{1,0:T(1,128)S(1)}, f32[1,1024]{1,0:T(1,128)}, u32[]{:S(2)}) copy-start(f32[1,1024]{1,0:T(1,128)} %copy-done.22) | copy-start | bytes 12292
  341.5 56.8 %copy-start.4 = (f32[256,1024]{1,0:T(8,128)S(1)}, f32[256,1024]{1,0:T(8,128)}, u32[]{:S(2)}) copy-start(f32[256,1024]{1,0:T(8,128)} %get-tuple-element.296) | copy-start | bytes 3145732
  (29 other events, 193.1 us)
Sparse Core Ops, SparseCore 0:
  14.2 33.3 all-gather.6
  281.9 32.9 all-gather.8
where the time goes:
time: 487 us; the launch traced here: 480 us
  local copies, waits for them, and re-layouts  218 us (45%)
  blocking collectives  98 us (20%)
  other arithmetic  79.8 us (16%)
  waiting for transfers between devices  35.2 us (7%)
  matrix products  24.5 us (5%)
  between operations  14.8 us (3%)
  starting transfers between devices  6.89 us (1%)
    slice x104, local copies, waits for them, and re-layouts, per_device(): gains, shifts = lax.associative_scan(compose, (slope, offset), axis=0)  140 us
    all_gather x4, blocking collectives, prefix(): pieces = jax.tree.map(lambda part: lax.all_gather(part, axis), value)  98 us
    pad x56, local copies, waits for them, and re-layouts, per_device(): gains, shifts = lax.associative_scan(compose, (slope, offset), axis=0)  45.2 us
    all_gather x2, waiting for transfers between devices, per_device(): lax.all_gather(previous.astype(jnp.bfloat16), 'hid', axis=1, tiled=True)  34.4 us
    mul x26, other arithmetic, compose(): return (later_gain * earlier_gain, later_gain * earlier_shift + later_shift)  32.1 us
    dot_general x2, matrix products, per_device(): jnp.einsum('tk,gko->tgo', piece, weight_rows, preferred_element_type=jnp....  24.5 us
    concatenate x27, other arithmetic, per_device(): gains, shifts = lax.associative_scan(compose, (slope, offset), axis=0)  14.6 us
    add x27, other arithmetic, per_device(): gains, shifts = lax.associative_scan(compose, (slope, offset), axis=0)  13.4 us
  transfers between devices with their start and end apart: 4, of which 3 were waited for; matrix products, arithmetic and copies ran while one was open for 7% of the time, Pallas kernels for 0%

commit v1 on v0

--- a/solution.py
+++ b/solution.py
@@ -50,7 +50,27 @@
         incoming = jnp.where(time_index == 0, initial_state, boundary_row(states))
         previous = jnp.concatenate([incoming[None, :], states[:-1]], axis=0)
         empty = jnp.zeros((rows, 3, own), jnp.float32)
-        piece = lax.all_gather(previous.astype(jnp.bfloat16), "hid", axis=1, tiled=True)
+        value_2 = previous.astype(jnp.bfloat16)
+        length, here, rows_2 = (lax.axis_size("hid"), lax.axis_index("hid"), value_2.shape[1])
+        upward = [(i_2, (i_2 + 1) % length) for i_2 in range(length)]
+        behind = [(i_2, (i_2 - 1) % length) for i_2 in range(length)]
+        filled = jnp.zeros(
+            (*value_2.shape[:1], length * rows_2, *value_2.shape[1 + 1 :]), value_2.dtype
+        )
+        filled = lax.dynamic_update_slice_in_dim(filled, value_2, here * rows_2, axis=1)
+        from_left = from_right = value_2
+        half = length // 2
+        for step_2 in range(1, half + 1):
+            from_left = lax.ppermute(from_left, "hid", upward)
+            filled = lax.dynamic_update_slice_in_dim(
+                filled, from_left, (here - step_2) % length * rows_2, axis=1
+            )
+            if step_2 < length - half:
+                from_right = lax.ppermute(from_right, "hid", behind)
+                filled = lax.dynamic_update_slice_in_dim(
+                    filled, from_right, (here + step_2) % length * rows_2, axis=1
+                )
+        piece = filled
         weight_rows = lax.slice_in_dim(recurrent, 0, piece.shape[1], axis=1)
         total = empty + jnp.einsum(
             "tk,gko->tgo", piece, weight_rows, preferred_element_type=jnp.float32

time: 487 us -> 486 us (level)
  between operations: 14.8 us -> 1.4 us
  local copies, waits for them, and re-layouts: 218 us -> 228 us
  starting transfers between devices: 6.89 us -> 13.3 us
    all_gather x2 -> x0, waiting for transfers between devices: 34.4 us -> none  [per_device(): lax.all_gather(previous.astype(jnp.bfloat16), 'hid', axis=1, tiled=True)]
    ppermute x0 -> x6, waiting for transfers between devices: none -> 31.2 us  [the longest x4 23.5 us: per_device(): from_left = lax.ppermute(from_left, 'hid', upward)]
    dynamic_update_slice x0 -> x6, local copies, waits for them, and re-layouts: none -> 11.5 us  [the longest x4 7.64 us: per_device(): lax.dynamic_update_slice_in_dim(filled, from_left, (here - step_2) % leng...]
    ppermute x0 -> x6, starting transfers between devices: none -> 6.52 us  [the longest x2 4.65 us: per_device(): from_right = lax.ppermute(from_right, 'hid', behind)]
  transfers between devices with their start and end apart: 4 -> 8, of which waited for: 3 -> 5; matrix products, arithmetic and copies ran while one was open for 7% -> 8% of each run, Pallas kernels for 0% -> 0%
where the time goes in v1:
time: 486 us; the launch traced here: 479 us
  local copies, waits for them, and re-layouts  228 us (47%)
  blocking collectives  96.7 us (20%)
  other arithmetic  80.1 us (16%)
  waiting for transfers between devices  32 us (7%)
  matrix products  24.5 us (5%)
  starting transfers between devices  13.3 us (3%)
    slice x104, local copies, waits for them, and re-layouts, per_device(): gains, shifts = lax.associative_scan(compose, (slope, offset), axis=0)  135 us
    all_gather x4, blocking collectives, prefix(): pieces = jax.tree.map(lambda part: lax.all_gather(part, axis), value)  96.7 us
    pad x56, local copies, waits for them, and re-layouts, per_device(): gains, shifts = lax.associative_scan(compose, (slope, offset), axis=0)  44.4 us
    mul x26, other arithmetic, compose(): return (later_gain * earlier_gain, later_gain * earlier_shift + later_shift)  30.5 us
    dot_general x2, matrix products, per_device(): jnp.einsum('tk,gko->tgo', piece, weight_rows, preferred_element_type=jnp....  24.5 us
    ppermute x4, waiting for transfers between devices, per_device(): from_left = lax.ppermute(from_left, 'hid', upward)  23.5 us
    concatenate x27, other arithmetic, per_device(): gains, shifts = lax.associative_scan(compose, (slope, offset), axis=0)  16.6 us
    unnamed x103, local copies, waits for them, and re-layouts  16 us
  transfers between devices with their start and end apart: 8, of which 5 were waited for; matrix products, arithmetic and copies ran while one was open for 8% of the time, Pallas kernels for 0%

profile of v1, /device:TPU:1, one launch (start us, length us, event | category | flops | bytes accessed | tf_op | source)
XLA Modules:
  0.0 478.7 jit_solution(2321718321772560847)
XLA Ops:
  0.7 4.5 collective-permute-start
  10.6 6.1 %constant_dynamic-slice_fusion.4 = bf16[3,1024,1024]{2,1,0:T(8,128)(2,1)} fusion(bf16[3,4096,1024]{2,1,0:T(8,128)(2,1)} %param.9, s32[]{:T(128)S(6)} %select_n.112), kind=kLoop, calls=%fused_computation.194 | loop fusion | bytes 12582916 | tf_op jit(solution)/shard_map/dynamic_slice | solution.py:44
  16.7 11.5 %copy.12 = bf16[3,1024,1024]{2,0,1:T(4,128)(2,1)} copy(bf16[3,1024,1024]{2,1,0:T(8,128)(2,1)} %constant_dynamic-slice_fusion.4) | data formatting | bytes 12582912
  28.3 12.3 %gather_fusion = bf16[1024,3]{0,1:T(4,128)(2,1)S(1)} fusion(bf16[3,1024,1024]{2,0,1:T(4,128)(2,1)} %copy.12, s32[1024]{0:T(1024)S(1)} %bitcast.117), kind=kCustom, calls=%fused_computation | custom fusion | bytes 20480 | tf_op jit(solution)/shard_map/jit(diagonal)/gather | solution.py:45
  46.6 7.7 %collective-permute-done.2 = bf16[256,1024]{1,0:T(8,128)(2,1)} collective-permute-done((bf16[256,1024]{1,0:T(8,128)(2,1)}, bf16[256,1024]{1,0:T(8,128)(2,1)}, u32[]{:S(2)}, u32[]{:S(2)}) %collective-permute-start.2) | collective-permute-done | bytes 524320 | tf_op jit(solution)/shard_map/ppermute | solution.py:69
  59.3 12.3 %fusion.2 = f32[256,3,1024]{2,0,1:T(8,128)S(1)} fusion(bf16[3,4096,1024]{2,1,0:T(8,128)(2,1)} %param.9, bf16[256,4096]{1,0:T(8,128)(2,1)} %constant_dynamic-update-slice_fusion.4), kind=kOutput, calls=%fused_computation.11 | convolution fusion | flops 6442450944 | bytes 30408704 | tf_op jit(solution)/shard_map/tk,gko->tgo/dot_general | solution.py:75
  74.2 3.3 slice.539
  77.5 3.3 slice.540
  80.8 3.3 slice.576
  84.0 3.3 slice.577
  158.9 3.3 slice.538
  162.2 3.3 slice.611
  202.0 4.6 pad.227
  218.4 4.6 pad.226
  223.8 25.7 %all-gather.1 = f32[32,1,1024]{2,1,0:T(1,128)S(1)} all-gather(f32[1,1,1024]{2,1,0:T(1,128)S(1)} %add_bitcast_fusion.2), channel_id=1, replica_groups=mesh['tm'=32,'hid'=4] {'tm'}, dimensions={0}, use_global_device_ids=true | all-gather | bytes 135168 | tf_op jit(solution)/shard_map/all_gather | solution.py:17
  249.5 4.6 pad.211
  256.0 4.7 pad.210
  261.5 23.0 %all-gather = f32[32,1,1024]{2,1,0:T(1,128)S(1)} all-gather(f32[1,1,1024]{2,1,0:T(1,128)S(1)} %add_bitcast_fusion.3), channel_id=1, replica_groups=mesh['tm'=32,'hid'=4] {'tm'}, dimensions={0}, use_global_device_ids=true | all-gather | bytes 135168 | tf_op jit(solution)/shard_map/all_gather | solution.py:17
  297.2 12.2 %collective-permute-done.5 = bf16[256,1024]{1,0:T(8,128)(2,1)} collective-permute-done((bf16[256,1024]{1,0:T(8,128)(2,1)}, bf16[256,1024]{1,0:T(8,128)(2,1)}, u32[]{:S(2)}, u32[]{:S(2)}) %collective-permute-start.5) | collective-permute-done | bytes 524320 | tf_op jit(solution)/shard_map/ppermute | solution.py:64
  313.3 10.1 %collective-permute-done.7 = bf16[256,1024]{1,0:T(8,128)(2,1)} collective-permute-done((bf16[256,1024]{1,0:T(8,128)(2,1)}, bf16[256,1024]{1,0:T(8,128)(2,1)}, u32[]{:S(2)}, u32[]{:S(2)}) %collective-permute-start.7) | collective-permute-done | bytes 524320 | tf_op jit(solution)/shard_map/ppermute | solution.py:64
  325.3 12.3 %fusion = f32[256,3,1024]{2,0,1:T(8,128)S(1)} fusion(bf16[3,4096,1024]{2,1,0:T(8,128)(2,1)} %param.9, bf16[256,4096]{1,0:T(8,128)(2,1)} %constant_dynamic-update-slice_fusion), kind=kOutput, calls=%fused_computation.9 | convolution fusion | flops 6442450944 | bytes 30408704 | tf_op jit(solution)/shard_map/tk,gko->tgo/dot_general | solution.py:75
  416.9 26.1 %all-gather.3 = f32[32,1,1024]{2,1,0:T(1,128)S(1)} all-gather(f32[1,1,1024]{2,1,0:T(1,128)S(1)} %add_bitcast_fusion), channel_id=1, replica_groups=mesh['tm'=32,'hid'=4] {'tm'}, dimensions={0}, use_global_device_ids=true | all-gather | bytes 135168 | tf_op jit(solution)/shard_map/all_gather | solution.py:17
  447.0 4.6 pad.242
  452.4 22.0 %all-gather.2 = f32[32,1,1024]{2,1,0:T(1,128)S(1)} all-gather(f32[1,1,1024]{2,1,0:T(1,128)S(1)} %add_bitcast_fusion.1), channel_id=1, replica_groups=mesh['tm'=32,'hid'=4] {'tm'}, dimensions={0}, use_global_device_ids=true | all-gather | bytes 135168 | tf_op jit(solution)/shard_map/all_gather | solution.py:17
  (506 shorter events, 250.2 us)
Async XLA Ops:
  0.7 5.7 %collective-permute-start = (f32[1024]{0:T(1024)S(1)}, f32[1024]{0:T(1024)S(1)}, u32[]{:S(2)}, u32[]{:S(2)}) collective-permute-start(f32[1024]{0:T(1024)S(1)} %bitcast.138), channel_id=1, source_target_pairs={{0,4},{4,8},{8,12},{12,16},{16,20},{20,24},{24,28},{28,32},{32,36}... | collective-permute-start | bytes 12296 | tf_op jit(solution)/shard_map/ppermute | solution.py:12
  9.0 33.8 %collective-permute-start.1 = (bf16[256,1024]{1,0:T(8,128)(2,1)}, bf16[256,1024]{1,0:T(8,128)(2,1)}, u32[]{:S(2)}, u32[]{:S(2)}) collective-permute-start(bf16[256,1024]{1,0:T(8,128)(2,1)} %get-tuple-element.302), channel_id=1, source_target_pairs={{0,1},{1,2},{2,3},{3,0},{4,5},{5,6},{6,7},{7,4},{8,9},{9,10},{10,1... | collective-permute-start | bytes 1572872 | tf_op jit(solution)/shard_map/ppermute | solution.py:64
  40.6 13.8 %collective-permute-start.2 = (bf16[256,1024]{1,0:T(8,128)(2,1)}, bf16[256,1024]{1,0:T(8,128)(2,1)}, u32[]{:S(2)}, u32[]{:S(2)}) collective-permute-start(bf16[256,1024]{1,0:T(8,128)(2,1)} %get-tuple-element.302), channel_id=1, source_target_pairs={{0,3},{1,0},{2,1},{3,2},{4,7},{5,4},{6,5},{7,6},{8,11},{9,8},{10,9... | collective-permute-start | bytes 1572872 | tf_op jit(solution)/shard_map/ppermute | solution.py:69
  42.8 14.7 %collective-permute-start.3 = (bf16[256,1024]{1,0:T(8,128)(2,1)}, bf16[256,1024]{1,0:T(8,128)(2,1)}, u32[]{:S(2)}, u32[]{:S(2)}) collective-permute-start(bf16[256,1024]{1,0:T(8,128)(2,1)} %collective-permute-done.1), channel_id=1, source_target_pairs={{0,1},{1,2},{2,3},{3,0},{4,5},{5,6},{6,7},{7,4},{8,9},{9,10},{10,1... | collective-permute-start | bytes 1572872 | tf_op jit(solution)/shard_map/ppermute | solution.py:64
  44.7 26.9 %copy-start.25 = (f32[1,1024]{1,0:T(1,128)}, f32[1,1024]{1,0:T(1,128)S(1)}, u32[]{:S(2)}) copy-start(f32[1,1024]{1,0:T(1,128)S(1)} %get-tuple-element.368) | copy-start | bytes 12292
  44.7 26.9 %copy-start.27 = (f32[1,1024]{1,0:T(1,128)}, f32[1,1024]{1,0:T(1,128)S(1)}, u32[]{:S(2)}) copy-start(f32[1,1024]{1,0:T(1,128)S(1)} %get-tuple-element.369) | copy-start | bytes 12292
  149.1 20.3 %copy-start.16 = (f32[7,1024]{1,0:T(8,128)S(1)}, f32[7,1024]{1,0:T(8,128)}, u32[]{:S(2)}) copy-start(f32[7,1024]{1,0:T(8,128)} %slice.554) | copy-start | bytes 86020
  149.1 20.3 %copy-start.17 = (f32[7,1024]{1,0:T(8,128)S(1)}, f32[7,1024]{1,0:T(8,128)}, u32[]{:S(2)}) copy-start(f32[7,1024]{1,0:T(8,128)} %slice.603) | copy-start | bytes 86020
  152.7 15.6 %copy-start.32 = (f32[2,1024]{1,0:T(2,128)S(1)}, f32[2,1024]{1,0:T(2,128)}, u32[]{:S(2)}) copy-start(f32[2,1024]{1,0:T(2,128)} %get-tuple-element.383) | copy-start | bytes 24580
  152.7 15.6 %copy-start.31 = (f32[2,1024]{1,0:T(2,128)S(1)}, f32[2,1024]{1,0:T(2,128)}, u32[]{:S(2)}) copy-start(f32[2,1024]{1,0:T(2,128)} %get-tuple-element.382) | copy-start | bytes 24580
  152.7 15.6 %copy-start.45 = (f32[1,1024]{1,0:T(1,128)S(1)}, f32[1,1024]{1,0:T(1,128)}, u32[]{:S(2)}) copy-start(f32[1,1024]{1,0:T(1,128)} %get-tuple-element.361) | copy-start | bytes 12292
  152.7 15.6 %copy-start.46 = (f32[1,1024]{1,0:T(1,128)S(1)}, f32[1,1024]{1,0:T(1,128)}, u32[]{:S(2)}) copy-start(f32[1,1024]{1,0:T(1,128)} %get-tuple-element.362) | copy-start | bytes 12292
  152.7 15.6 %copy-start.47 = (f32[1,1024]{1,0:T(1,128)S(1)}, f32[1,1024]{1,0:T(1,128)}, u32[]{:S(2)}) copy-start(f32[1,1024]{1,0:T(1,128)} %get-tuple-element.363) | copy-start | bytes 12292
  152.7 15.6 %copy-start.48 = (f32[1,1024]{1,0:T(1,128)S(1)}, f32[1,1024]{1,0:T(1,128)}, u32[]{:S(2)}) copy-start(f32[1,1024]{1,0:T(1,128)} %get-tuple-element.364) | copy-start | bytes 12292
  152.7 15.7 %copy-start.21 = (f32[3,1024]{1,0:T(4,128)S(1)}, f32[3,1024]{1,0:T(4,128)}, u32[]{:S(2)}) copy-start(f32[3,1024]{1,0:T(4,128)} %slice.558) | copy-start | bytes 36868
  152.7 15.7 %copy-start.22 = (f32[3,1024]{1,0:T(4,128)S(1)}, f32[3,1024]{1,0:T(4,128)}, u32[]{:S(2)}) copy-start(f32[3,1024]{1,0:T(4,128)} %slice.601) | copy-start | bytes 36868
  152.7 15.8 %copy-start.44 = (f32[1,1024]{1,0:T(1,128)S(1)}, f32[1,1024]{1,0:T(1,128)}, u32[]{:S(2)}) copy-start(f32[1,1024]{1,0:T(1,128)} %slice.738) | copy-start | bytes 12292
  156.2 15.3 %copy-start.13 = (f32[15,1024]{1,0:T(8,128)S(1)}, f32[15,1024]{1,0:T(8,128)}, u32[]{:S(2)}) copy-start(f32[15,1024]{1,0:T(8,128)} %slice.550) | copy-start | bytes 184324
  217.6 36.6 %copy-start.33 = (f32[1,1024]{1,0:T(1,128)S(1)}, f32[1,1024]{1,0:T(1,128)}, u32[]{:S(2)}) copy-start(f32[1,1024]{1,0:T(1,128)} %slice.707) | copy-start | bytes 12292
  289.0 3.1 collective-permute-start.4
  294.6 14.9 %collective-permute-start.5 = (bf16[256,1024]{1,0:T(8,128)(2,1)}, bf16[256,1024]{1,0:T(8,128)(2,1)}, u32[]{:S(2)}, u32[]{:S(2)}) collective-permute-start(bf16[256,1024]{1,0:T(8,128)(2,1)} %get-tuple-element.298), channel_id=1, source_target_pairs={{0,1},{1,2},{2,3},{3,0},{4,5},{5,6},{6,7},{7,4},{8,9},{9,10},{10,1... | collective-permute-start | bytes 1572872 | tf_op jit(solution)/shard_map/ppermute | solution.py:64
  294.8 16.6 %collective-permute-start.6 = (bf16[256,1024]{1,0:T(8,128)(2,1)}, bf16[256,1024]{1,0:T(8,128)(2,1)}, u32[]{:S(2)}, u32[]{:S(2)}) collective-permute-start(bf16[256,1024]{1,0:T(8,128)(2,1)} %get-tuple-element.298), channel_id=1, source_target_pairs={{0,3},{1,0},{2,1},{3,2},{4,7},{5,4},{6,5},{7,6},{8,11},{9,8},{10,9... | collective-permute-start | bytes 1572872 | tf_op jit(solution)/shard_map/ppermute | solution.py:69
  309.5 14.0 %collective-permute-start.7 = (bf16[256,1024]{1,0:T(8,128)(2,1)}, bf16[256,1024]{1,0:T(8,128)(2,1)}, u32[]{:S(2)}, u32[]{:S(2)}) collective-permute-start(bf16[256,1024]{1,0:T(8,128)(2,1)} %collective-permute-done.5), channel_id=1, source_target_pairs={{0,1},{1,2},{2,3},{3,0},{4,5},{5,6},{6,7},{7,4},{8,9},{9,10},{10,1... | collective-permute-start | bytes 1572872 | tf_op jit(solution)/shard_map/ppermute | solution.py:64
  352.4 50.3 %copy-start.4 = (f32[256,1024]{1,0:T(8,128)S(1)}, f32[256,1024]{1,0:T(8,128)}, u32[]{:S(2)}) copy-start(f32[256,1024]{1,0:T(8,128)} %get-tuple-element.296) | copy-start | bytes 3145732
  (33 other events, 188.3 us)
